TPU v7x, 32 devices: a whole 2x2x4 slice. The times are simulated.
32 devices in a mesh: rows: 16 (over z, x, core), rhs: 2 (over y).
Axes of the slice: x: 2, y: 2, z: 4, core: 2. Of those that a mesh axis runs over, the one named last changes fastest.
Arguments:
- obs_points: int32 [2, 1, 8192], P(None, None, 'rows'), may hold values from 0 to 255
- pred_points: int32 [2, 2048], P(None, 'rhs'), may hold values from 0 to 255
- factor_panels: bfloat16 [1, 8192, 2, 512], P(None, ('rows', 'rhs')), may hold values from -0.25 to 0.25
- diag_inverse: bfloat16 [2, 512, 512], P(None, 'rhs'), as said below
Outputs:
- updated: bfloat16 [1, 8192, 2048], P(None, 'rows', 'rhs')
Inputs may be any that keep to these rules, and one draw needn't show every extreme that they name: `diag_inverse`: lower triangular.
All inputs are finite; a program needn't handle non-finite values.
Results may differ from a plain program's by a relative error of at most 0.006.
Values may be sent and summed in bfloat16 or wider, within the bound.
A program may use at most 64 MiB of HBM per device.

v0:
```python
import math

import jax
import jax.numpy as jnp
from jax import lax
from jax.sharding import PartitionSpec as P

SCALE = 16


sill_level = 8.0


def spread(block, axis, holder):
    block = jnp.where(lax.axis_index(axis) == holder, block, jnp.zeros_like(block))
    return lax.psum(block, axis)


def covariance(points, targets):
    delta_x = points[0][..., None] - targets[0]
    delta_y = points[1][..., None] - targets[1]
    distance = jnp.sqrt(delta_x * delta_x + delta_y * delta_y)
    scaled = math.sqrt(3.0) / SCALE * distance
    return sill_level * (1.0 + scaled) * jnp.exp(-scaled)


def solve_block(inverse, rhs_block):
    return jnp.dot(
        inverse, rhs_block.astype(jnp.bfloat16), preferred_element_type=jnp.float32
    ).astype(jnp.bfloat16)


def apply_tiles(tiles, solved):
    return jnp.einsum("sab,bp->sap", tiles, solved, preferred_element_type=jnp.float32)


def on_device(obs_points, pred_points, factor_panels, diag_inverse):
    position = lax.axis_index("rows")
    panels, inverses = (
        lax.all_gather(factor_panels, "rhs", axis=1, tiled=True),
        lax.all_gather(diag_inverse, "rhs", axis=1, tiled=True),
    )
    targets = pred_points.astype(jnp.float32)
    kernel_rows = covariance(obs_points.astype(jnp.float32), targets)
    empty_block = jnp.zeros((kernel_rows.shape[1], kernel_rows.shape[2]), jnp.bfloat16)
    own_first = lax.cond(
        position == 0, lambda: solve_block(inverses[0], kernel_rows[0]), lambda: empty_block
    )
    first_solved = spread(own_first, "rows", 0)
    partial_value = kernel_rows - apply_tiles(panels[:, :, 0, :], first_solved)
    own_second = lax.cond(
        position == 1, lambda: solve_block(inverses[1], partial_value[0]), lambda: empty_block
    )
    second_solved = spread(own_second, "rows", 1)
    remain = partial_value - apply_tiles(panels[:, :, 1, :], second_solved)
    result = remain.astype(jnp.bfloat16)
    leading_row = jnp.where(
        position == 0, first_solved, jnp.where(position == 1, second_solved, result[0])
    )
    return result.at[0].set(leading_row)


def solution(mesh):
    in_specs = (
        P(None, None, "rows"),
        P(None, "rhs"),
        P(None, ("rows", "rhs"), None, None),
        P(None, "rhs", None),
    )
    out_specs = P(None, "rows", "rhs")
    return jax.shard_map(
        on_device, mesh=mesh, in_specs=in_specs, out_specs=out_specs, check_vma=False
    )
```

profile of v0, /device:TPU:9, one launch (start us, length us, event | category | flops | bytes accessed | tf_op | source)
XLA Modules:
  0.0 258.1 jit_solution(13588396174627132035)
XLA Ops:
  6.5 0.0 all-gather.3.cloned.1.call-start
  6.5 0.7 all-gather.3.cloned.1.call-update
  7.3 0.0 all-gather.5.cloned.1.call-start
  7.3 1.9 copy.8
  9.2 0.0 all-gather.5.cloned.1.call-update
  9.2 0.0 all-reduce.3.cloned.1.call-start
  9.3 0.0 copy-done.1
  9.3 0.0 copy-done
  9.4 22.0 %all-gather.3.cloned.1.call-done = bf16[2,512,512]{2,1,0:T(8,128)(2,1)} async-done(((bf16[2,256,512]{2,1,0:T(8,128)(2,1)}), bf16[2,512,512]{2,1,0:T(8,128)(2,1)}) %all-gather.3.cloned.1.call-update) | async-done | bytes 1048592 | tf_op jit(solution)/shard_map/all_gather | solution.py:41
  31.4 0.1 conditional.2
  31.4 0.1 broadcast.168
  31.5 1.0 broadcast_select_fusion.1
  32.5 0.0 all-reduce.3.cloned.1.call-update
  32.6 0.0 all-reduce.5.cloned.1.call-start
  32.6 21.7 %all-gather.5.cloned.1.call-done = bf16[1,512,2,512]{3,1,2,0:T(8,128)(2,1)} async-done(((bf16[1,256,2,512]{3,1,2,0:T(8,128)(2,1)}), bf16[1,512,2,512]{3,1,2,0:T(8,128)(2,1)}) %all-gather.5.cloned.1.call-update) | async-done | bytes 1048592 | tf_op jit(solution)/shard_map/all_gather | solution.py:40
  54.3 94.9 %all-reduce.3.cloned.1.call-done = bf16[512,1024]{0,1:T(8,128)(2,1)} async-done(((bf16[512,1024]{0,1:T(8,128)(2,1)}), bf16[512,1024]{0,1:T(8,128)(2,1)}) %all-reduce.3.cloned.1.call-update) | async-done | bytes 1048592 | tf_op jit(solution)/shard_map/psum | solution.py:16
  149.2 3.1 %bitcast_subtract_fusion.1 = f32[512,1024]{0,1:T(8,128)S(1)} fusion(bf16[512,1024]{0,1:T(8,128)(2,1)} %all-reduce.3.cloned.1.call-done, f32[1024]{0:T(1024)S(1)} %bitcast.39, f32[512]{0:T(512)S(1)} %bitcast.43, f32[1024]{0:T(1024)S(1)} %bitcast.41, f32[512]{0:T(512)S(1)} %bitcast.45, bf16[1,512,2,512]{3,1,2,0:T(8,128)(2,1)} %all-gather.5.cloned.1.call-done), kind=kOutput, calls=%fused_computation.22 | convolution fusion | flops 542638080 | bytes 3682304 | tf_op jit(solution)/shard_map/sab,bp->sap/dot_general | solution.py:34
  152.3 0.1 conditional.3
  152.4 0.1 broadcast.169.clone
  152.4 1.0 broadcast_select_fusion
  153.5 0.0 all-reduce.5.cloned.1.call-update
  153.5 94.3 %all-reduce.5.cloned.1.call-done = bf16[512,1024]{0,1:T(8,128)(2,1)} async-done(((bf16[512,1024]{0,1:T(8,128)(2,1)}), bf16[512,1024]{0,1:T(8,128)(2,1)}) %all-reduce.5.cloned.1.call-update) | async-done | bytes 1048592 | tf_op jit(solution)/shard_map/psum | solution.py:16
  247.8 2.4 fusion.21
  250.2 1.3 copy.11
  (6 shorter events, 0.0 us)
Async XLA Ops:
  6.5 2.8 %copy-start.1 = (s32[2,1,512]{2,1,0:T(1,128)S(1)}, s32[2,1,512]{2,1,0:T(1,128)}, u32[]{:S(2)}) copy-start(s32[2,1,512]{2,1,0:T(1,128)} %param.10) | copy-start | bytes 12292
  6.5 2.8 %copy-start = (s32[2,1024]{1,0:T(2,128)S(1)}, s32[2,1024]{1,0:T(2,128)}, u32[]{:S(2)}) copy-start(s32[2,1024]{1,0:T(2,128)} %param.11) | copy-start | bytes 24580
  6.5 24.9 %all-gather.3.cloned.1.call-start = ((), (), s32[]{:S(2)}) async-start(), calls=%async_computation | async-start | bytes 1572864 | tf_op jit(solution)/shard_map/all_gather | solution.py:41
  7.3 47.0 %all-gather.5.cloned.1.call-start = ((), (), s32[]{:S(2)}) async-start(), calls=%async_computation.2 | async-start | bytes 1572864 | tf_op jit(solution)/shard_map/all_gather | solution.py:40
  9.2 140.0 %all-reduce.3.cloned.1.call-start = ((), (), s32[]{:S(2)}) async-start(), calls=%async_computation.1 | async-start | bytes 2097152 | tf_op jit(solution)/shard_map/psum | solution.py:16
  32.6 215.2 %all-reduce.5.cloned.1.call-start = ((), (), s32[]{:S(2)}) async-start(), calls=%async_computation.3 | async-start | bytes 2097152 | tf_op jit(solution)/shard_map/psum | solution.py:16
Sparse Core Ops, SparseCore 0:
  8.9 22.4 all-gather.2
  32.9 21.2 all-gather.4
  57.8 91.4 all-reduce.2
  153.6 94.0 all-reduce.4
where the time goes:
time: 262 us; the launch traced here: 258 us
  waiting for transfers between devices  234 us (89%)
  between operations  13.2 us (5%)
  matrix products  5.54 us (2%)
  local copies, waits for them, and re-layouts  3.38 us (1%)
    psum x2, waiting for transfers between devices, spread(): return lax.psum(block, axis)  189 us
    all_gather x1, waiting for transfers between devices, on_device(): lax.all_gather(diag_inverse, 'rhs', axis=1, tiled=True)  22 us
    all_gather x1, waiting for transfers between devices, on_device(): lax.all_gather(factor_panels, 'rhs', axis=1, tiled=True)  21.7 us
    dot_general x2, matrix products, apply_tiles(): jnp.einsum('sab,bp->sap', tiles, solved, preferred_element_type=jnp.float32)  5.54 us
  transfers between devices with their start and end apart: 4, of which 4 were waited for; matrix products, arithmetic and copies ran while one was open for 1% of the time, Pallas kernels for 0%

commit v1 on v0

v1 whole, which is shorter than its diff:
```python
import functools
import math

import jax
import jax.numpy as jnp
from jax import lax
from jax.experimental import pallas as pl
from jax.experimental.pallas import tpu as pltpu
from jax.sharding import PartitionSpec as P

SCALE = 16
SILL = 8.0
LANES = 4
PIECES = 2
RATE = math.sqrt(3.0) / SCALE * math.log2(math.e)
SLOPE = SILL * math.log(2.0)
MESH = pl.DeviceIdType.MESH


def covariance(px, py, ox, oy):
    dx = ox - px
    dy = oy - py
    square = dx * dx + dy * dy
    scaled = (square * RATE) * lax.rsqrt(jnp.maximum(square, 1e-6))
    return (SILL + SLOPE * scaled) * jnp.exp2(-scaled)


def kernel(
    n_rows, n_rhs, obs_ref, pred_ref, panel_ref, inv_ref, out_ref,
    head, tiles, solved, base, first_rhs, second_base, lead_pts, columns, result,
    local_sem, send_sem, recv_sem,
):
    r = lax.axis_index("rows")
    c = lax.axis_index("rhs")
    bs = head.shape[1]
    q = bs // n_rhs
    w = q // LANES
    lane = lax.rem(r, LANES)
    hop = r // LANES
    hops = n_rows // LANES
    x_side = r + 2 - 4 * (lane // 2)
    c_side = r + 1 - 2 * lax.rem(lane, 2)
    x_lane = lax.rem(x_side, LANES)
    c_lane = lax.rem(c_side, LANES)
    d_lane = lax.rem(c_lane + 2, LANES)
    is_first = r == 0
    is_second = r == 1
    updates = r >= 2

    send_count = [0]
    recv_count = [0]

    def slot(count):
        count[0] += 1
        return count[0] - 1

    def link(src, dst, row, side, send=None, recv=None):
        return pltpu.make_async_remote_copy(
            src_ref=src, dst_ref=dst,
            send_sem=send_sem.at[slot(send_count) if send is None else send],
            recv_sem=recv_sem.at[slot(recv_count) if recv is None else recv],
            device_id=(row, side), device_id_type=MESH,
        )

    def rows_of(side, which):
        return pl.ds(pl.multiple_of(side * q + which * w, w), w)

    def chunk(side):
        return pl.ds(pl.multiple_of(side * q, q), q)

    own = chunk(c)
    copy_inv = pltpu.make_async_copy(inv_ref, head.at[0:2, own], local_sem.at[0])
    copy_tiles = pltpu.make_async_copy(panel_ref, tiles.at[:, own], local_sem.at[1])
    copy_lower = pltpu.make_async_copy(
        panel_ref.at[0, pl.ds(w, w)], head.at[2, rows_of(c, 1)], local_sem.at[2]
    )
    copy_inv.start()
    copy_tiles.start()

    @pl.when(is_second)
    def _():
        copy_lower.start()

    barrier = pltpu.get_barrier_semaphore()
    first_of_hop = hop * LANES
    for dl in range(LANES):
        for dc in range(n_rhs):
            if dl == 0 and dc == 0:
                continue
            pl.semaphore_signal(
                barrier, inc=1, device_id_type=MESH,
                device_id=(first_of_hop + lax.rem(lane + dl, LANES), lax.rem(c + dc, n_rhs)),
            )
    has_next = hop < hops - 1
    has_prev = hop > 0

    @pl.when(has_next)
    def _():
        pl.semaphore_signal(barrier, inc=1, device_id=(r + LANES, c), device_id_type=MESH)

    @pl.when(has_prev)
    def _():
        pl.semaphore_signal(barrier, inc=1, device_id=(r - LANES, c), device_id_type=MESH)

    neighbours = has_next.astype(jnp.int32) + has_prev.astype(jnp.int32)
    pl.semaphore_wait(barrier, LANES * n_rhs - 1 + neighbours)

    point_recv = [slot(recv_count) for _ in range(2)]
    point_copies = []
    for block in range(2):
        sends = []
        for other in range(LANES):
            if other != block:
                sends.append(link(obs_ref, lead_pts.at[block], other, c, recv=point_recv[block]))
        point_copies.append(sends)

        @pl.when(r == block)
        def _():
            for copy in sends:
                copy.start()

    inv_copies = []
    inv_recv = []
    for d in range(1, n_rhs):
        inv_recv.append(slot(recv_count))
        copy = link(
            inv_ref.at[:, pl.ds(pl.multiple_of(lane * w, w), w)], head.at[0:2, rows_of(c, lane)],
            r, lax.rem(c + d, n_rhs), recv=inv_recv[-1],
        )
        copy.start()
        inv_copies.append(copy)

    lower_recv = [slot(recv_count) for _ in range(n_rhs)]
    lower_copies = []
    for source in range(n_rhs):
        sends = []
        for other in range(LANES):
            for side in range(n_rhs):
                if (other, side) != (1, source):
                    sends.append(link(
                        panel_ref.at[0, pl.ds(other * w, w)],
                        head.at[2, pl.ds(source * q + other * w, w)],
                        other, side, recv=lower_recv[source],
                    ))
        lower_copies.append(sends)

        @pl.when(is_second & (c == source))
        def _():
            for copy in sends:
                copy.start()

    step = q // PIECES
    tile_copies = []
    tile_recv = []
    for piece in range(PIECES):
        for d in range(1, n_rhs):
            tile_recv.append(slot(recv_count))
            tile_copies.append(link(
                panel_ref.at[:, pl.ds(piece * step, step)],
                tiles.at[:, pl.ds(pl.multiple_of(c * q + piece * step, step), step)],
                r, lax.rem(c + d, n_rhs), recv=tile_recv[-1],
            ))

    @pl.when(updates)
    def _():
        for copy in tile_copies:
            copy.start()

    px = pred_ref[0:1, :].astype(jnp.float32)
    py = pred_ref[1:2, :].astype(jnp.float32)
    pick = lax.broadcasted_iota(jnp.int32, (8, bs), 0) == 0
    strip = 32

    def cover(points, store, low, high):
        ox = jnp.broadcast_to(points[0], (8, bs)).astype(jnp.float32)
        oy = jnp.broadcast_to(points[1], (8, bs)).astype(jnp.float32)
        columns[...] = jnp.where(pick, ox, oy).T

        @pl.loop(low, high)
        def _(i):
            at = pl.ds(pl.multiple_of(i * strip, strip), strip)
            store(at, covariance(px, py, columns[at, 0:1], columns[at, 1:2]))

    def put_base(at, value):
        base[at, :] = value

    def put_first(at, value):
        first_rhs[at, :] = value.astype(jnp.bfloat16)

    def put_second(at, value):
        second_base[at, :] = value

    strips = bs // strip
    forwards = []

    def forward(src, row, recv):
        copy = link(src, src, row, c, recv=recv)
        forwards.append(copy)
        return copy

    def arrived(dst, recv):
        link(dst, dst, r, lax.rem(c + 1, n_rhs), send=0, recv=recv).wait_recv()

    chain_copies = []

    def along_chain(src, recv):
        copy = link(src, src, r + LANES, c, recv=recv)
        chain_copies.append(copy)

        @pl.when(has_next)
        def _():
            copy.start()

    for block in range(2):
        @pl.when(r != block)
        def _():
            arrived(lead_pts.at[block], point_recv[block])

        @pl.when(r == block)
        def _():
            copy = pltpu.make_async_copy(obs_ref, lead_pts.at[block], local_sem.at[3])
            copy.start()
            copy.wait()

        along_chain(lead_pts.at[block], point_recv[block])

    @pl.when(updates)
    def _():
        cover(obs_ref, put_base, 0, strips // 2)

    inv_from = [lax.rem(c + n_rhs - d, n_rhs) for d in range(1, n_rhs)]
    inv_x = [slot(recv_count) for _ in inv_from]
    inv_c = [slot(recv_count) for _ in inv_from]
    inv_xc = [slot(recv_count) for _ in inv_from]
    for k, side in enumerate(inv_from):
        part = head.at[0:2, rows_of(side, lane)]
        arrived(part, inv_recv[k])
        forward(part, x_side, inv_x[k]).start()
        forward(part, c_side, inv_c[k]).start()

    lower_x = [slot(recv_count) for _ in range(n_rhs)]
    lower_c = [slot(recv_count) for _ in range(n_rhs)]
    lower_xc = [slot(recv_count) for _ in range(n_rhs)]
    for side in range(n_rhs):
        part = head.at[2, rows_of(side, lane)]
        here = is_second & (c == side)

        @pl.when(jnp.logical_not(here))
        def _():
            arrived(part, lower_recv[side])

        @pl.when(here)
        def _():
            copy_lower.wait()

        along_chain(part, lower_recv[side])
        forward(part, x_side, lower_x[side]).start()
        forward(part, c_side, lower_c[side]).start()

    cover(lead_pts.at[0], put_first, 0, strips)

    for k, side in enumerate(inv_from):
        part = head.at[0:2, rows_of(side, x_lane)]
        arrived(part, inv_x[k])
        forward(part, c_side, inv_xc[k]).start()

    cover(lead_pts.at[1], put_second, 0, strips)

    for side in range(n_rhs):
        part = head.at[2, rows_of(side, x_lane)]
        arrived(part, lower_x[side])
        forward(part, c_side, lower_xc[side]).start()

    @pl.when(updates)
    def _():
        cover(obs_ref, put_base, strips // 2, strips)

    for k, side in enumerate(inv_from):
        arrived(head.at[0:2, rows_of(side, c_lane)], inv_c[k])
        arrived(head.at[0:2, rows_of(side, d_lane)], inv_xc[k])
    copy_inv.wait()

    half = solved.shape[2] // 2
    for n in range(2):
        at = slice(n * half, (n + 1) * half)
        solved[0, :, at] = jnp.dot(
            head[0], first_rhs[:, at], preferred_element_type=jnp.float32
        ).astype(jnp.bfloat16)

    for side in range(n_rhs):
        arrived(head.at[2, rows_of(side, c_lane)], lower_c[side])
        arrived(head.at[2, rows_of(side, d_lane)], lower_xc[side])

    for n in range(2):
        at = slice(n * half, (n + 1) * half)
        second_rhs = (second_base[:, at] - jnp.dot(
            head[2], solved[0, :, at], preferred_element_type=jnp.float32
        )).astype(jnp.bfloat16)
        solved[1, :, at] = jnp.dot(
            head[1], second_rhs, preferred_element_type=jnp.float32
        ).astype(jnp.bfloat16)

    copy_tiles.wait()

    def update(at, sem):
        total = base[at, :] - jnp.dot(tiles[0, at, :], solved[0], preferred_element_type=jnp.float32)
        total = total - jnp.dot(tiles[1, at, :], solved[1], preferred_element_type=jnp.float32)
        result[at, :] = total.astype(jnp.bfloat16)
        copy = pltpu.make_async_copy(result.at[at], out_ref.at[0, at], local_sem.at[sem])
        copy.start()
        return copy

    for block in range(2):
        @pl.when(r == block)
        def _():
            copy = pltpu.make_async_copy(solved.at[block], out_ref.at[0], local_sem.at[4])
            copy.start()
            copy.wait()

    @pl.when(updates)
    def _():
        writes = [update(own, 4)]
        sem = 5
        count = 0
        for piece in range(PIECES):
            for d in range(1, n_rhs):
                side = lax.rem(c + n_rhs - d, n_rhs)
                at = pl.ds(pl.multiple_of(side * q + piece * step, step), step)
                arrived(tiles.at[:, at], tile_recv[count])
                writes.append(update(at, sem))
                count += 1
                sem += 1
        for copy in writes:
            copy.wait()
        for copy in tile_copies:
            copy.wait_send()

    for block in range(2):
        @pl.when(r == block)
        def _():
            for copy in point_copies[block]:
                copy.wait_send()
    for copy in inv_copies + forwards:
        copy.wait_send()
    for source in range(n_rhs):
        @pl.when(is_second & (c == source))
        def _():
            for copy in lower_copies[source]:
                copy.wait_send()

    @pl.when(has_next)
    def _():
        for copy in chain_copies:
            copy.wait_send()


def on_device(n_rows, n_rhs, obs_points, pred_points, factor_panels, diag_inverse):
    panels = jnp.transpose(factor_panels[0], (1, 0, 2))
    bs = obs_points.shape[2]
    cols = pred_points.shape[1]
    bf16, f32 = jnp.bfloat16, jnp.float32
    copies = 64 + 24 * n_rhs * n_rhs
    return pl.pallas_call(
        functools.partial(kernel, n_rows, n_rhs),
        out_shape=jax.ShapeDtypeStruct((1, bs, cols), bf16),
        in_specs=[
            pl.BlockSpec(memory_space=pltpu.VMEM),
            pl.BlockSpec(memory_space=pltpu.VMEM),
            pl.BlockSpec(memory_space=pl.ANY),
            pl.BlockSpec(memory_space=pl.ANY),
        ],
        out_specs=pl.BlockSpec(memory_space=pl.ANY),
        scratch_shapes=[
            pltpu.VMEM((3, bs, bs), bf16),
            pltpu.VMEM((2, bs, bs), bf16),
            pltpu.VMEM((2, bs, cols), bf16),
            pltpu.VMEM((bs, cols), f32),
            pltpu.VMEM((bs, cols), bf16),
            pltpu.VMEM((bs, cols), f32),
            pltpu.VMEM((2,) + obs_points.shape, jnp.int32),
            pltpu.VMEM((bs, 8), f32),
            pltpu.VMEM((bs, cols), bf16),
            pltpu.SemaphoreType.DMA((8 + PIECES * n_rhs,)),
            pltpu.SemaphoreType.DMA((copies,)),
            pltpu.SemaphoreType.DMA((copies,)),
        ],
        compiler_params=pltpu.CompilerParams(
            collective_id=0, has_side_effects=True, vmem_limit_bytes=40 * 1024 * 1024
        ),
        cost_estimate=pl.CostEstimate(
            flops=10 * bs * bs * cols, bytes_accessed=4 * bs * cols, transcendentals=6 * bs * cols
        ),
    )(obs_points, pred_points, panels, diag_inverse)


def solution(mesh):
    in_specs = (
        P(None, None, "rows"),
        P(None, "rhs"),
        P(None, ("rows", "rhs"), None, None),
        P(None, "rhs", None),
    )
    body = functools.partial(on_device, mesh.shape["rows"], mesh.shape["rhs"])
    return jax.shard_map(
        body, mesh=mesh, in_specs=in_specs, out_specs=P(None, "rows", "rhs"), check_vma=False
    )
```

time: 262 us -> 33.2 us (0.13)
  the two profiles are of different devices: /device:TPU:9 before, /device:TPU:28 now
where the time goes in v1:
time: 33.2 us; the launch traced here: 33.1 us
  Pallas kernels  30.9 us (93%)
  local copies, waits for them, and re-layouts  2.17 us (7%)
    pallas_call x1, Pallas kernels, on_device(): pl.pallas_call(functools.partial(kernel, n_rows, n_rhs), out_shape=jax.Sh...  30.9 us
    unnamed x8, local copies, waits for them, and re-layouts  2.17 us

profile of v1, /device:TPU:28, one launch (start us, length us, event | category | flops | bytes accessed | tf_op | source)
XLA Modules:
  0.0 33.1 jit_solution(11021349623215585258)
XLA Ops:
  0.0 0.0 copy-start
  0.0 0.0 copy-start.1
  0.0 0.0 copy-start.2
  0.0 1.2 %copy.7 = bf16[1,256,2,512]{3,1,2,0:T(8,128)(2,1)S(1)} copy(bf16[1,256,2,512]{3,2,1,0:T(2,128)(2,1)} %param.6) | data formatting | bytes 1048576 | tf_op args[2]
  1.2 0.0 copy-done
  1.2 0.0 copy-done.1
  1.2 0.0 copy-done.2
  1.2 30.9 %shard_map.46 = bf16[1,512,1024]{2,1,0:T(8,128)(2,1)S(1)} custom-call(s32[2,1,512]{2,1,0:T(1,128)S(1)} %copy-done.2, s32[2,1024]{1,0:T(2,128)S(1)} %copy-done.1, bf16[2,256,512]{2,1,0:T(8,128)(2,1)S(1)} %bitcast.5, bf16[2,256,512]{2,1,0:T(8,128)(2,1)S(1)} %copy-done), custom_call_target="tpu_custom_call" | custom-call | flops 2684354560 | bytes 2097152 | tf_op jit(solution)/shard_map/pallas_call | solution.py:363
  32.1 1.0 %copy.9 = bf16[1,512,1024]{2,1,0:T(8,128)(2,1)} copy(bf16[1,512,1024]{2,1,0:T(8,128)(2,1)S(1)} %shard_map.46) | data formatting | bytes 2097152
Async XLA Ops:
  0.0 1.2 %copy-start = (bf16[2,256,512]{2,1,0:T(8,128)(2,1)S(1)}, bf16[2,256,512]{2,1,0:T(8,128)(2,1)}, u32[]{:S(2)}) copy-start(bf16[2,256,512]{2,1,0:T(8,128)(2,1)} %inv_ref.1) | copy-start | bytes 1572868
  0.0 1.2 %copy-start.1 = (s32[2,1024]{1,0:T(2,128)S(1)}, s32[2,1024]{1,0:T(2,128)}, u32[]{:S(2)}) copy-start(s32[2,1024]{1,0:T(2,128)} %pred_ref.1) | copy-start | bytes 24580
  0.0 1.2 %copy-start.2 = (s32[2,1,512]{2,1,0:T(1,128)S(1)}, s32[2,1,512]{2,1,0:T(1,128)}, u32[]{:S(2)}) copy-start(s32[2,1,512]{2,1,0:T(1,128)} %obs_ref.1) | copy-start | bytes 12292

commit v2 on v1

--- a/solution.py
+++ b/solution.py
@@ -28,7 +28,7 @@
 def kernel(
     n_rows, n_rhs, obs_ref, pred_ref, panel_ref, inv_ref, out_ref,
     head, tiles, solved, base, first_rhs, second_base, lead_pts, columns, result,
-    local_sem, send_sem, recv_sem,
+    local_sem, send_sem, recv_sem, spread_sem, point_sem,
 ):
     r = lax.axis_index("rows")
     c = lax.axis_index("rhs")
@@ -36,8 +36,6 @@
     q = bs // n_rhs
     w = q // LANES
     lane = lax.rem(r, LANES)
-    hop = r // LANES
-    hops = n_rows // LANES
     x_side = r + 2 - 4 * (lane // 2)
     c_side = r + 1 - 2 * lax.rem(lane, 2)
     x_lane = lax.rem(x_side, LANES)
@@ -82,72 +80,91 @@
         copy_lower.start()
 
     barrier = pltpu.get_barrier_semaphore()
-    first_of_hop = hop * LANES
-    for dl in range(LANES):
-        for dc in range(n_rhs):
-            if dl == 0 and dc == 0:
-                continue
-            pl.semaphore_signal(
-                barrier, inc=1, device_id_type=MESH,
-                device_id=(first_of_hop + lax.rem(lane + dl, LANES), lax.rem(c + dc, n_rhs)),
-            )
-    has_next = hop < hops - 1
-    has_prev = hop > 0
-
-    @pl.when(has_next)
-    def _():
-        pl.semaphore_signal(barrier, inc=1, device_id=(r + LANES, c), device_id_type=MESH)
-
-    @pl.when(has_prev)
-    def _():
-        pl.semaphore_signal(barrier, inc=1, device_id=(r - LANES, c), device_id_type=MESH)
-
-    neighbours = has_next.astype(jnp.int32) + has_prev.astype(jnp.int32)
-    pl.semaphore_wait(barrier, LANES * n_rhs - 1 + neighbours)
-
-    point_recv = [slot(recv_count) for _ in range(2)]
-    point_copies = []
-    for block in range(2):
-        sends = []
-        for other in range(LANES):
-            if other != block:
-                sends.append(link(obs_ref, lead_pts.at[block], other, c, recv=point_recv[block]))
-        point_copies.append(sends)
-
-        @pl.when(r == block)
-        def _():
-            for copy in sends:
-                copy.start()
+
+    def greet(row, side):
+        pl.semaphore_signal(barrier, inc=1, device_id=(row, side), device_id_type=MESH)
+
+    for d in range(1, n_rhs):
+        greet(r, lax.rem(c + d, n_rhs))
+    greet(x_side, c)
+    greet(c_side, c)
+
+    @pl.when(r != 0)
+    def _():
+        greet(0, c)
+
+    for side in range(n_rhs):
+        @pl.when(jnp.logical_not(is_second & (c == side)))
+        def _():
+            greet(1, side)
+
+    pl.semaphore_wait(
+        barrier,
+        n_rhs + 1
+        + is_first.astype(jnp.int32) * (n_rows - 1)
+        + is_second.astype(jnp.int32) * (n_rows * n_rhs - 1),
+    )
 
     inv_copies = []
     inv_recv = []
-    for d in range(1, n_rhs):
-        inv_recv.append(slot(recv_count))
-        copy = link(
-            inv_ref.at[:, pl.ds(pl.multiple_of(lane * w, w), w)], head.at[0:2, rows_of(c, lane)],
-            r, lax.rem(c + d, n_rhs), recv=inv_recv[-1],
+    for k in range(2):
+        for d in range(1, n_rhs):
+            inv_recv.append(slot(recv_count))
+            copy = link(
+                inv_ref.at[k, pl.ds(pl.multiple_of(lane * w, w), w)], head.at[k, rows_of(c, lane)],
+                r, lax.rem(c + d, n_rhs), recv=inv_recv[-1],
+            )
+            copy.start()
+            inv_copies.append(copy)
+
+    point_recv = [slot(recv_count) for _ in range(2)]
+
+    def point_copy(block, row):
+        return pltpu.make_async_remote_copy(
+            src_ref=obs_ref, dst_ref=lead_pts.at[block], send_sem=point_sem.at[row],
+            recv_sem=recv_sem.at[point_recv[block]], device_id=(row, c), device_id_type=MESH,
         )
-        copy.start()
-        inv_copies.append(copy)
+
+    def each_point(block, act):
+        @pl.when(r == block)
+        def _():
+            @pl.loop(0, n_rows)
+            def _(row):
+                @pl.when(row != block)
+                def _():
+                    act(point_copy(block, row))
+
+    for block in range(2):
+        each_point(block, lambda copy: copy.start())
 
     lower_recv = [slot(recv_count) for _ in range(n_rhs)]
-    lower_copies = []
-    for source in range(n_rhs):
-        sends = []
-        for other in range(LANES):
-            for side in range(n_rhs):
-                if (other, side) != (1, source):
-                    sends.append(link(
-                        panel_ref.at[0, pl.ds(other * w, w)],
-                        head.at[2, pl.ds(source * q + other * w, w)],
-                        other, side, recv=lower_recv[source],
-                    ))
-        lower_copies.append(sends)
-
-        @pl.when(is_second & (c == source))
-        def _():
-            for copy in sends:
-                copy.start()
+
+    def lower_copy(source, row, side):
+        which = lax.rem(row, LANES)
+        return pltpu.make_async_remote_copy(
+            src_ref=panel_ref.at[0, pl.ds(pl.multiple_of(which * w, w), w)],
+            dst_ref=head.at[2, rows_of(source, which)],
+            send_sem=spread_sem.at[row * n_rhs + side],
+            recv_sem=recv_sem.at[lower_recv[source]],
+            device_id=(row, side), device_id_type=MESH,
+        )
+
+    def each_lower(act):
+        for source in range(n_rhs):
+            @pl.when(is_second & (c == source))
+            def _():
+                @pl.loop(0, n_rows)
+                def _(back):
+                    row = n_rows - 1 - back
+                    for side in range(n_rhs):
+                        if side == source:
+                            @pl.when(row != 1)
+                            def _():
+                                act(lower_copy(source, row, side))
+                        else:
+                            act(lower_copy(source, row, side))
+
+    each_lower(lambda copy: copy.start())
 
     step = q // PIECES
     tile_copies = []
@@ -201,15 +218,21 @@
     def arrived(dst, recv):
         link(dst, dst, r, lax.rem(c + 1, n_rhs), send=0, recv=recv).wait_recv()
 
-    chain_copies = []
-
-    def along_chain(src, recv):
-        copy = link(src, src, r + LANES, c, recv=recv)
-        chain_copies.append(copy)
-
-        @pl.when(has_next)
-        def _():
-            copy.start()
+    @pl.when(updates)
+    def _():
+        cover(obs_ref, put_base, 0, strips // 2)
+
+    inv_from = [
+        (k, lax.rem(c + n_rhs - d, n_rhs)) for k in range(2) for d in range(1, n_rhs)
+    ]
+    inv_x = [slot(recv_count) for _ in inv_from]
+    inv_c = [slot(recv_count) for _ in inv_from]
+    inv_xc = [slot(recv_count) for _ in inv_from]
+    for n, (k, side) in enumerate(inv_from):
+        part = head.at[k, rows_of(side, lane)]
+        arrived(part, inv_recv[n])
+        forward(part, x_side, inv_x[n]).start()
+        forward(part, c_side, inv_c[n]).start()
 
     for block in range(2):
         @pl.when(r != block)
@@ -222,21 +245,12 @@
             copy.start()
             copy.wait()
 
-        along_chain(lead_pts.at[block], point_recv[block])
-
-    @pl.when(updates)
-    def _():
-        cover(obs_ref, put_base, 0, strips // 2)
-
-    inv_from = [lax.rem(c + n_rhs - d, n_rhs) for d in range(1, n_rhs)]
-    inv_x = [slot(recv_count) for _ in inv_from]
-    inv_c = [slot(recv_count) for _ in inv_from]
-    inv_xc = [slot(recv_count) for _ in inv_from]
-    for k, side in enumerate(inv_from):
-        part = head.at[0:2, rows_of(side, lane)]
-        arrived(part, inv_recv[k])
-        forward(part, x_side, inv_x[k]).start()
-        forward(part, c_side, inv_c[k]).start()
+    cover(lead_pts.at[0], put_first, 0, strips)
+
+    for n, (k, side) in enumerate(inv_from):
+        part = head.at[k, rows_of(side, x_lane)]
+        arrived(part, inv_x[n])
+        forward(part, c_side, inv_xc[n]).start()
 
     lower_x = [slot(recv_count) for _ in range(n_rhs)]
     lower_c = [slot(recv_count) for _ in range(n_rhs)]
@@ -253,16 +267,8 @@
         def _():
             copy_lower.wait()
 
-        along_chain(part, lower_recv[side])
         forward(part, x_side, lower_x[side]).start()
         forward(part, c_side, lower_c[side]).start()
-
-    cover(lead_pts.at[0], put_first, 0, strips)
-
-    for k, side in enumerate(inv_from):
-        part = head.at[0:2, rows_of(side, x_lane)]
-        arrived(part, inv_x[k])
-        forward(part, c_side, inv_xc[k]).start()
 
     cover(lead_pts.at[1], put_second, 0, strips)
 
@@ -275,11 +281,15 @@
     def _():
         cover(obs_ref, put_base, strips // 2, strips)
 
-    for k, side in enumerate(inv_from):
-        arrived(head.at[0:2, rows_of(side, c_lane)], inv_c[k])
-        arrived(head.at[0:2, rows_of(side, d_lane)], inv_xc[k])
     copy_inv.wait()
 
+    def inverse_here(block):
+        for n, (k, side) in enumerate(inv_from):
+            if k == block:
+                arrived(head.at[k, rows_of(side, c_lane)], inv_c[n])
+                arrived(head.at[k, rows_of(side, d_lane)], inv_xc[n])
+
+    inverse_here(0)
     half = solved.shape[2] // 2
     for n in range(2):
         at = slice(n * half, (n + 1) * half)
@@ -290,6 +300,7 @@
     for side in range(n_rhs):
         arrived(head.at[2, rows_of(side, c_lane)], lower_c[side])
         arrived(head.at[2, rows_of(side, d_lane)], lower_xc[side])
+    inverse_here(1)
 
     for n in range(2):
         at = slice(n * half, (n + 1) * half)
@@ -336,22 +347,10 @@
             copy.wait_send()
 
     for block in range(2):
-        @pl.when(r == block)
-        def _():
-            for copy in point_copies[block]:
-                copy.wait_send()
+        each_point(block, lambda copy: copy.wait_send())
     for copy in inv_copies + forwards:
         copy.wait_send()
-    for source in range(n_rhs):
-        @pl.when(is_second & (c == source))
-        def _():
-            for copy in lower_copies[source]:
-                copy.wait_send()
-
-    @pl.when(has_next)
-    def _():
-        for copy in chain_copies:
-            copy.wait_send()
+    each_lower(lambda copy: copy.wait_send())
 
 
 def on_device(n_rows, n_rhs, obs_points, pred_points, factor_panels, diag_inverse):
@@ -359,7 +358,7 @@
     bs = obs_points.shape[2]
     cols = pred_points.shape[1]
     bf16, f32 = jnp.bfloat16, jnp.float32
-    copies = 64 + 24 * n_rhs * n_rhs
+    copies = 16 + 20 * n_rhs
     return pl.pallas_call(
         functools.partial(kernel, n_rows, n_rhs),
         out_shape=jax.ShapeDtypeStruct((1, bs, cols), bf16),
@@ -383,6 +382,8 @@
             pltpu.SemaphoreType.DMA((8 + PIECES * n_rhs,)),
             pltpu.SemaphoreType.DMA((copies,)),
             pltpu.SemaphoreType.DMA((copies,)),
+            pltpu.SemaphoreType.DMA((n_rows * n_rhs,)),
+            pltpu.SemaphoreType.DMA((n_rows,)),
         ],
         compiler_params=pltpu.CompilerParams(
             collective_id=0, has_side_effects=True, vmem_limit_bytes=40 * 1024 * 1024

time: 33.2 us -> 36.9 us (1.11)
  the two profiles are of different devices: /device:TPU:28 before, /device:TPU:14 now
where the time goes in v2:
time: 36.9 us; the launch traced here: 36.8 us
  Pallas kernels  34.6 us (94%)
  local copies, waits for them, and re-layouts  2.17 us (6%)
    pallas_call x1, Pallas kernels, on_device(): pl.pallas_call(functools.partial(kernel, n_rows, n_rhs), out_shape=jax.Sh...  34.6 us
    unnamed x8, local copies, waits for them, and re-layouts  2.17 us

profile of v2, /device:TPU:14, one launch (start us, length us, event | category | flops | bytes accessed | tf_op | source)
XLA Modules:
  0.0 36.8 jit_solution(132585731356552784)
XLA Ops:
  0.0 0.0 copy-start
  0.0 0.0 copy-start.1
  0.0 0.0 copy-start.2
  0.0 1.2 %copy.7 = bf16[1,256,2,512]{3,1,2,0:T(8,128)(2,1)S(1)} copy(bf16[1,256,2,512]{3,2,1,0:T(2,128)(2,1)} %param.6) | data formatting | bytes 1048576 | tf_op args[2]
  1.2 0.0 copy-done
  1.2 0.0 copy-done.1
  1.2 0.0 copy-done.2
  1.2 34.6 %shard_map.46 = bf16[1,512,1024]{2,1,0:T(8,128)(2,1)S(1)} custom-call(s32[2,1,512]{2,1,0:T(1,128)S(1)} %copy-done.2, s32[2,1024]{1,0:T(2,128)S(1)} %copy-done.1, bf16[2,256,512]{2,1,0:T(8,128)(2,1)S(1)} %bitcast.5, bf16[2,256,512]{2,1,0:T(8,128)(2,1)S(1)} %copy-done), custom_call_target="tpu_custom_call" | custom-call | flops 2684354560 | bytes 2097152 | tf_op jit(solution)/shard_map/pallas_call | solution.py:362
  35.8 1.0 %copy.9 = bf16[1,512,1024]{2,1,0:T(8,128)(2,1)} copy(bf16[1,512,1024]{2,1,0:T(8,128)(2,1)S(1)} %shard_map.46) | data formatting | bytes 2097152
Async XLA Ops:
  0.0 1.2 %copy-start = (bf16[2,256,512]{2,1,0:T(8,128)(2,1)S(1)}, bf16[2,256,512]{2,1,0:T(8,128)(2,1)}, u32[]{:S(2)}) copy-start(bf16[2,256,512]{2,1,0:T(8,128)(2,1)} %inv_ref.1) | copy-start | bytes 1572868
  0.0 1.2 %copy-start.1 = (s32[2,1024]{1,0:T(2,128)S(1)}, s32[2,1024]{1,0:T(2,128)}, u32[]{:S(2)}) copy-start(s32[2,1024]{1,0:T(2,128)} %pred_ref.1) | copy-start | bytes 24580
  0.0 1.2 %copy-start.2 = (s32[2,1,512]{2,1,0:T(1,128)S(1)}, s32[2,1,512]{2,1,0:T(1,128)}, u32[]{:S(2)}) copy-start(s32[2,1,512]{2,1,0:T(1,128)} %obs_ref.1) | copy-start | bytes 12292

commit v3 on v2

--- a/solution.py
+++ b/solution.py
@@ -28,7 +28,7 @@
 def kernel(
     n_rows, n_rhs, obs_ref, pred_ref, panel_ref, inv_ref, out_ref,
     head, tiles, solved, base, first_rhs, second_base, lead_pts, columns, result,
-    local_sem, send_sem, recv_sem, spread_sem, point_sem,
+    local_sem, send_sem, recv_sem,
 ):
     r = lax.axis_index("rows")
     c = lax.axis_index("rhs")
@@ -36,6 +36,10 @@
     q = bs // n_rhs
     w = q // LANES
     lane = lax.rem(r, LANES)
+    hop = r // LANES
+    hops = n_rows // LANES
+    has_next = hop < hops - 1
+    has_prev = hop > 0
     x_side = r + 2 - 4 * (lane // 2)
     c_side = r + 1 - 2 * lax.rem(lane, 2)
     x_lane = lax.rem(x_side, LANES)
@@ -86,23 +90,30 @@
 
     for d in range(1, n_rhs):
         greet(r, lax.rem(c + d, n_rhs))
-    greet(x_side, c)
-    greet(c_side, c)
-
-    @pl.when(r != 0)
-    def _():
-        greet(0, c)
-
-    for side in range(n_rhs):
-        @pl.when(jnp.logical_not(is_second & (c == side)))
-        def _():
-            greet(1, side)
+    mates = [hop * LANES + lax.rem(lane + d, LANES) for d in range(1, LANES)]
+    for mate in mates:
+        greet(mate, c)
+    passes_points = lane < 2
+
+    @pl.when(has_prev)
+    def _():
+        greet(r - LANES, c)
+
+    @pl.when(has_prev & passes_points)
+    def _():
+        greet(lane, c)
+
+    @pl.when(hop == 0)
+    def _():
+        for d in range(1, n_rhs):
+            greet(1, lax.rem(c + d, n_rhs))
 
     pl.semaphore_wait(
         barrier,
-        n_rhs + 1
-        + is_first.astype(jnp.int32) * (n_rows - 1)
-        + is_second.astype(jnp.int32) * (n_rows * n_rhs - 1),
+        n_rhs + LANES - 2
+        + has_next.astype(jnp.int32)
+        + (r < 2).astype(jnp.int32) * (hops - 1)
+        + is_second.astype(jnp.int32) * (LANES * (n_rhs - 1)),
     )
 
     inv_copies = []
@@ -118,53 +129,41 @@
             inv_copies.append(copy)
 
     point_recv = [slot(recv_count) for _ in range(2)]
-
-    def point_copy(block, row):
-        return pltpu.make_async_remote_copy(
-            src_ref=obs_ref, dst_ref=lead_pts.at[block], send_sem=point_sem.at[row],
-            recv_sem=recv_sem.at[point_recv[block]], device_id=(row, c), device_id_type=MESH,
-        )
-
-    def each_point(block, act):
+    far_copies = []
+    for block in range(2):
+        sends = [
+            link(obs_ref, lead_pts.at[block], block + LANES * h, c, recv=point_recv[block])
+            for h in range(1, hops)
+        ]
+        far_copies.append(sends)
+
         @pl.when(r == block)
         def _():
-            @pl.loop(0, n_rows)
-            def _(row):
-                @pl.when(row != block)
-                def _():
-                    act(point_copy(block, row))
-
-    for block in range(2):
-        each_point(block, lambda copy: copy.start())
+            for copy in sends:
+                copy.start()
+    mate_copies = [
+        [link(lead_pts.at[block], lead_pts.at[block], mate, c, recv=point_recv[block]) for mate in mates]
+        for block in range(2)
+    ]
 
     lower_recv = [slot(recv_count) for _ in range(n_rhs)]
-
-    def lower_copy(source, row, side):
-        which = lax.rem(row, LANES)
-        return pltpu.make_async_remote_copy(
-            src_ref=panel_ref.at[0, pl.ds(pl.multiple_of(which * w, w), w)],
-            dst_ref=head.at[2, rows_of(source, which)],
-            send_sem=spread_sem.at[row * n_rhs + side],
-            recv_sem=recv_sem.at[lower_recv[source]],
-            device_id=(row, side), device_id_type=MESH,
-        )
-
-    def each_lower(act):
-        for source in range(n_rhs):
-            @pl.when(is_second & (c == source))
-            def _():
-                @pl.loop(0, n_rows)
-                def _(back):
-                    row = n_rows - 1 - back
-                    for side in range(n_rhs):
-                        if side == source:
-                            @pl.when(row != 1)
-                            def _():
-                                act(lower_copy(source, row, side))
-                        else:
-                            act(lower_copy(source, row, side))
-
-    each_lower(lambda copy: copy.start())
+    lower_copies = []
+    for source in range(n_rhs):
+        sends = []
+        for other in range(LANES):
+            for side in range(n_rhs):
+                if (other, side) != (1, source):
+                    sends.append(link(
+                        panel_ref.at[0, pl.ds(other * w, w)],
+                        head.at[2, pl.ds(source * q + other * w, w)],
+                        other, side, recv=lower_recv[source],
+                    ))
+        lower_copies.append(sends)
+
+        @pl.when(is_second & (c == source))
+        def _():
+            for copy in sends:
+                copy.start()
 
     step = q // PIECES
     tile_copies = []
@@ -185,18 +184,20 @@
 
     px = pred_ref[0:1, :].astype(jnp.float32)
     py = pred_ref[1:2, :].astype(jnp.float32)
-    pick = lax.broadcasted_iota(jnp.int32, (8, bs), 0) == 0
     strip = 32
+    width = 2 * bs // 8
+    groups = bs // width
 
     def cover(points, store, low, high):
-        ox = jnp.broadcast_to(points[0], (8, bs)).astype(jnp.float32)
-        oy = jnp.broadcast_to(points[1], (8, bs)).astype(jnp.float32)
-        columns[...] = jnp.where(pick, ox, oy).T
-
-        @pl.loop(low, high)
-        def _(i):
-            at = pl.ds(pl.multiple_of(i * strip, strip), strip)
-            store(at, covariance(px, py, columns[at, 0:1], columns[at, 1:2]))
+        columns[...] = points[...].astype(jnp.float32).T
+        for g in range(low, high):
+            @pl.loop(0, width // strip)
+            def _(i):
+                part = pl.ds(pl.multiple_of(i * strip, strip), strip)
+                at = pl.ds(pl.multiple_of(g * width + i * strip, strip), strip)
+                ox = columns[part, g:g + 1]
+                oy = columns[part, groups + g:groups + g + 1]
+                store(at, covariance(px, py, ox, oy))
 
     def put_base(at, value):
         base[at, :] = value
@@ -207,7 +208,6 @@
     def put_second(at, value):
         second_base[at, :] = value
 
-    strips = bs // strip
     forwards = []
 
     def forward(src, row, recv):
@@ -218,9 +218,71 @@
     def arrived(dst, recv):
         link(dst, dst, r, lax.rem(c + 1, n_rhs), send=0, recv=recv).wait_recv()
 
+    def points_here(block):
+        @pl.when(r == block)
+        def _():
+            copy = pltpu.make_async_copy(obs_ref, lead_pts.at[block], local_sem.at[3])
+            copy.start()
+            copy.wait()
+
+        @pl.when(r != block)
+        def _():
+            arrived(lead_pts.at[block], point_recv[block])
+
+        @pl.when(lane == block)
+        def _():
+            for copy in mate_copies[block]:
+                copy.start()
+
+    lower_send = [[slot(send_count) for _ in range(3)] for _ in range(n_rhs)]
+    lower_x = [slot(recv_count) for _ in range(n_rhs)]
+    lower_c = [slot(recv_count) for _ in range(n_rhs)]
+    lower_xc = [slot(recv_count) for _ in range(n_rhs)]
+
+    def lower_links(side):
+        part = head.at[2, rows_of(side, lane)]
+        sends = lower_send[side]
+        return (
+            link(part, part, r + LANES, c, send=sends[0], recv=lower_recv[side]),
+            link(part, part, x_side, c, send=sends[1], recv=lower_x[side]),
+            link(part, part, c_side, c, send=sends[2], recv=lower_c[side]),
+        )
+
+    def lower_step(turn):
+        @pl.when(turn)
+        def _():
+            for side in range(n_rhs):
+                part = head.at[2, rows_of(side, lane)]
+                here = is_second & (c == side)
+
+                @pl.when(jnp.logical_not(here))
+                def _():
+                    arrived(part, lower_recv[side])
+
+                @pl.when(here)
+                def _():
+                    copy_lower.wait()
+
+                on, across, beside = lower_links(side)
+
+                @pl.when(has_next)
+                def _():
+                    on.start()
+
+                across.start()
+                beside.start()
+
+    @pl.when(passes_points)
+    def _():
+        for block in range(2):
+            @pl.when(lane == block)
+            def _():
+                points_here(block)
+    lower_step(hop == 0)
+
     @pl.when(updates)
     def _():
-        cover(obs_ref, put_base, 0, strips // 2)
+        cover(obs_ref, put_base, 0, groups // 2)
 
     inv_from = [
         (k, lax.rem(c + n_rhs - d, n_rhs)) for k in range(2) for d in range(1, n_rhs)
@@ -233,53 +295,23 @@
         arrived(part, inv_recv[n])
         forward(part, x_side, inv_x[n]).start()
         forward(part, c_side, inv_c[n]).start()
+    lower_step(hop == 1)
 
     for block in range(2):
-        @pl.when(r != block)
+        @pl.when(lane != block)
         def _():
             arrived(lead_pts.at[block], point_recv[block])
 
-        @pl.when(r == block)
-        def _():
-            copy = pltpu.make_async_copy(obs_ref, lead_pts.at[block], local_sem.at[3])
-            copy.start()
-            copy.wait()
-
-    cover(lead_pts.at[0], put_first, 0, strips)
+    cover(lead_pts.at[0], put_first, 0, groups)
 
     for n, (k, side) in enumerate(inv_from):
         part = head.at[k, rows_of(side, x_lane)]
         arrived(part, inv_x[n])
         forward(part, c_side, inv_xc[n]).start()
-
-    lower_x = [slot(recv_count) for _ in range(n_rhs)]
-    lower_c = [slot(recv_count) for _ in range(n_rhs)]
-    lower_xc = [slot(recv_count) for _ in range(n_rhs)]
-    for side in range(n_rhs):
-        part = head.at[2, rows_of(side, lane)]
-        here = is_second & (c == side)
-
-        @pl.when(jnp.logical_not(here))
-        def _():
-            arrived(part, lower_recv[side])
-
-        @pl.when(here)
-        def _():
-            copy_lower.wait()
-
-        forward(part, x_side, lower_x[side]).start()
-        forward(part, c_side, lower_c[side]).start()
-
-    cover(lead_pts.at[1], put_second, 0, strips)
-
-    for side in range(n_rhs):
-        part = head.at[2, rows_of(side, x_lane)]
-        arrived(part, lower_x[side])
-        forward(part, c_side, lower_xc[side]).start()
-
-    @pl.when(updates)
-    def _():
-        cover(obs_ref, put_base, strips // 2, strips)
+    lower_step(hop == 2)
+
+    cover(lead_pts.at[1], put_second, 0, groups)
+    lower_step(hop >= 3)
 
     copy_inv.wait()
 
@@ -296,6 +328,15 @@
         solved[0, :, at] = jnp.dot(
             head[0], first_rhs[:, at], preferred_element_type=jnp.float32
         ).astype(jnp.bfloat16)
+
+    for side in range(n_rhs):
+        part = head.at[2, rows_of(side, x_lane)]
+        arrived(part, lower_x[side])
+        forward(part, c_side, lower_xc[side]).start()
+
+    @pl.when(updates)
+    def _():
+        cover(obs_ref, put_base, groups // 2, groups)
 
     for side in range(n_rhs):
         arrived(head.at[2, rows_of(side, c_lane)], lower_c[side])
@@ -347,10 +388,31 @@
             copy.wait_send()
 
     for block in range(2):
-        each_point(block, lambda copy: copy.wait_send())
+        @pl.when(r == block)
+        def _():
+            for copy in far_copies[block]:
+                copy.wait_send()
+
+        @pl.when(lane == block)
+        def _():
+            for copy in mate_copies[block]:
+                copy.wait_send()
     for copy in inv_copies + forwards:
         copy.wait_send()
-    each_lower(lambda copy: copy.wait_send())
+    for source in range(n_rhs):
+        @pl.when(is_second & (c == source))
+        def _():
+            for copy in lower_copies[source]:
+                copy.wait_send()
+    for side in range(n_rhs):
+        on, across, beside = lower_links(side)
+
+        @pl.when(has_next)
+        def _():
+            on.wait_send()
+
+        across.wait_send()
+        beside.wait_send()
 
 
 def on_device(n_rows, n_rhs, obs_points, pred_points, factor_panels, diag_inverse):
@@ -358,7 +420,7 @@
     bs = obs_points.shape[2]
     cols = pred_points.shape[1]
     bf16, f32 = jnp.bfloat16, jnp.float32
-    copies = 16 + 20 * n_rhs
+    copies = 32 + 2 * n_rows + 16 * n_rhs + LANES * n_rhs * n_rhs
     return pl.pallas_call(
         functools.partial(kernel, n_rows, n_rhs),
         out_shape=jax.ShapeDtypeStruct((1, bs, cols), bf16),
@@ -376,14 +438,12 @@
             pltpu.VMEM((bs, cols), f32),
             pltpu.VMEM((bs, cols), bf16),
             pltpu.VMEM((bs, cols), f32),
-            pltpu.VMEM((2,) + obs_points.shape, jnp.int32),
-            pltpu.VMEM((bs, 8), f32),
+            pltpu.VMEM((2, 8, 2 * bs // 8), jnp.int32),
+            pltpu.VMEM((2 * bs // 8, 8), f32),
             pltpu.VMEM((bs, cols), bf16),
             pltpu.SemaphoreType.DMA((8 + PIECES * n_rhs,)),
             pltpu.SemaphoreType.DMA((copies,)),
             pltpu.SemaphoreType.DMA((copies,)),
-            pltpu.SemaphoreType.DMA((n_rows * n_rhs,)),
-            pltpu.SemaphoreType.DMA((n_rows,)),
         ],
         compiler_params=pltpu.CompilerParams(
             collective_id=0, has_side_effects=True, vmem_limit_bytes=40 * 1024 * 1024
@@ -391,7 +451,7 @@
         cost_estimate=pl.CostEstimate(
             flops=10 * bs * bs * cols, bytes_accessed=4 * bs * cols, transcendentals=6 * bs * cols
         ),
-    )(obs_points, pred_points, panels, diag_inverse)
+    )(obs_points.reshape(8, 2 * bs // 8), pred_points, panels, diag_inverse)
 
 
 def solution(mesh):

time: 36.9 us -> 30.3 us (0.82)
  the two profiles are of different devices: /device:TPU:14 before, /device:TPU:31 now
where the time goes in v3:
time: 30.3 us; the launch traced here: 30.1 us
  Pallas kernels  28 us (92%)
  local copies, waits for them, and re-layouts  2.17 us (7%)
    pallas_call x1, Pallas kernels, on_device(): pl.pallas_call(functools.partial(kernel, n_rows, n_rhs), out_shape=jax.Sh...  28 us
    unnamed x8, local copies, waits for them, and re-layouts  2.17 us

profile of v3, /device:TPU:31, one launch (start us, length us, event | category | flops | bytes accessed | tf_op | source)
XLA Modules:
  0.0 30.1 jit_solution(14120172287137188841)
XLA Ops:
  0.0 0.0 copy-start
  0.0 0.0 copy-start.1
  0.0 0.0 copy-start.2
  0.0 1.2 %copy.7 = bf16[1,256,2,512]{3,1,2,0:T(8,128)(2,1)S(1)} copy(bf16[1,256,2,512]{3,2,1,0:T(2,128)(2,1)} %param.6) | data formatting | bytes 1048576 | tf_op args[2]
  1.2 0.0 copy-done
  1.2 0.0 copy-done.1
  1.2 0.0 copy-done.2
  1.2 28.0 %shard_map.46 = bf16[1,512,1024]{2,1,0:T(8,128)(2,1)S(1)} custom-call(s32[8,128]{1,0:T(8,128)S(1)} %bitcast.7, s32[2,1024]{1,0:T(2,128)S(1)} %copy-done.1, bf16[2,256,512]{2,1,0:T(8,128)(2,1)S(1)} %bitcast.6, bf16[2,256,512]{2,1,0:T(8,128)(2,1)S(1)} %copy-done), custom_call_target="tpu_custom_call" | custom-call | flops 2684354560 | bytes 2097152 | tf_op jit(solution)/shard_map/pallas_call | solution.py:424
  29.2 1.0 %copy.9 = bf16[1,512,1024]{2,1,0:T(8,128)(2,1)} copy(bf16[1,512,1024]{2,1,0:T(8,128)(2,1)S(1)} %shard_map.46) | data formatting | bytes 2097152
Async XLA Ops:
  0.0 1.2 %copy-start = (bf16[2,256,512]{2,1,0:T(8,128)(2,1)S(1)}, bf16[2,256,512]{2,1,0:T(8,128)(2,1)}, u32[]{:S(2)}) copy-start(bf16[2,256,512]{2,1,0:T(8,128)(2,1)} %inv_ref.1) | copy-start | bytes 1572868
  0.0 1.2 %copy-start.1 = (s32[2,1024]{1,0:T(2,128)S(1)}, s32[2,1024]{1,0:T(2,128)}, u32[]{:S(2)}) copy-start(s32[2,1024]{1,0:T(2,128)} %pred_ref.1) | copy-start | bytes 24580
  0.0 1.2 %copy-start.2 = (s32[2,1,512]{2,1,0:T(1,128)S(1)}, s32[2,1,512]{2,1,0:T(1,128)}, u32[]{:S(2)}) copy-start(s32[2,1,512]{2,1,0:T(1,128)} %param.4) | copy-start | bytes 12292

commit v4 on v3

--- a/solution.py
+++ b/solution.py
@@ -38,8 +38,10 @@
     lane = lax.rem(r, LANES)
     hop = r // LANES
     hops = n_rows // LANES
-    has_next = hop < hops - 1
-    has_prev = hop > 0
+    middle = (hops + 1) // 2
+    depth = hop - middle * (hop >= middle).astype(jnp.int32) + (hop >= middle).astype(jnp.int32)
+    has_next = (hop < hops - 1) & (hop + 1 != middle)
+    has_prev = (hop > 0) & (hop != middle)
     x_side = r + 2 - 4 * (lane // 2)
     c_side = r + 1 - 2 * lax.rem(lane, 2)
     x_lane = lax.rem(x_side, LANES)
@@ -99,9 +101,14 @@
     def _():
         greet(r - LANES, c)
 
-    @pl.when(has_prev & passes_points)
+    @pl.when((hop > 0) & passes_points)
     def _():
         greet(lane, c)
+
+    @pl.when(hop == middle)
+    def _():
+        for side in range(n_rhs):
+            greet(1, side)
 
     @pl.when(hop == 0)
     def _():
@@ -113,7 +120,7 @@
         n_rhs + LANES - 2
         + has_next.astype(jnp.int32)
         + (r < 2).astype(jnp.int32) * (hops - 1)
-        + is_second.astype(jnp.int32) * (LANES * (n_rhs - 1)),
+        + is_second.astype(jnp.int32) * (LANES * (n_rhs - 1 + n_rhs)),
     )
 
     inv_copies = []
@@ -149,7 +156,14 @@
     lower_recv = [slot(recv_count) for _ in range(n_rhs)]
     lower_copies = []
     for source in range(n_rhs):
-        sends = []
+        sends = [
+            link(
+                panel_ref.at[0, pl.ds(other * w, w)],
+                head.at[2, pl.ds(source * q + other * w, w)],
+                middle * LANES + other, side, recv=lower_recv[source],
+            )
+            for other in range(LANES) for side in range(n_rhs)
+        ]
         for other in range(LANES):
             for side in range(n_rhs):
                 if (other, side) != (1, source):
@@ -278,7 +292,7 @@
             @pl.when(lane == block)
             def _():
                 points_here(block)
-    lower_step(hop == 0)
+    lower_step(depth == 0)
 
     @pl.when(updates)
     def _():
@@ -295,7 +309,7 @@
         arrived(part, inv_recv[n])
         forward(part, x_side, inv_x[n]).start()
         forward(part, c_side, inv_c[n]).start()
-    lower_step(hop == 1)
+    lower_step(depth == 1)
 
     for block in range(2):
         @pl.when(lane != block)
@@ -308,10 +322,10 @@
         part = head.at[k, rows_of(side, x_lane)]
         arrived(part, inv_x[n])
         forward(part, c_side, inv_xc[n]).start()
-    lower_step(hop == 2)
+    lower_step(depth == 2)
 
     cover(lead_pts.at[1], put_second, 0, groups)
-    lower_step(hop >= 3)
+    lower_step(depth >= 3)
 
     copy_inv.wait()
 
@@ -420,7 +434,7 @@
     bs = obs_points.shape[2]
     cols = pred_points.shape[1]
     bf16, f32 = jnp.bfloat16, jnp.float32
-    copies = 32 + 2 * n_rows + 16 * n_rhs + LANES * n_rhs * n_rhs
+    copies = 32 + 2 * n_rows + 16 * n_rhs + 2 * LANES * n_rhs * n_rhs
     return pl.pallas_call(
         functools.partial(kernel, n_rows, n_rhs),
         out_shape=jax.ShapeDtypeStruct((1, bs, cols), bf16),

time: 30.3 us -> 29.4 us (0.970)
  the two profiles are of different devices: /device:TPU:31 before, /device:TPU:9 now
where the time goes in v4:
time: 29.4 us; the launch traced here: 29.3 us
  Pallas kernels  27.1 us (92%)
  local copies, waits for them, and re-layouts  2.17 us (7%)
    pallas_call x1, Pallas kernels, on_device(): pl.pallas_call(functools.partial(kernel, n_rows, n_rhs), out_shape=jax.Sh...  27.1 us
    unnamed x8, local copies, waits for them, and re-layouts  2.17 us

profile of v4, /device:TPU:9, one launch (start us, length us, event | category | flops | bytes accessed | tf_op | source)
XLA Modules:
  0.0 29.3 jit_solution(9971859242728428318)
XLA Ops:
  0.0 0.0 copy-start
  0.0 0.0 copy-start.1
  0.0 0.0 copy-start.2
  0.0 1.2 %copy.7 = bf16[1,256,2,512]{3,1,2,0:T(8,128)(2,1)S(1)} copy(bf16[1,256,2,512]{3,2,1,0:T(2,128)(2,1)} %param.6) | data formatting | bytes 1048576 | tf_op args[2]
  1.2 0.0 copy-done
  1.2 0.0 copy-done.1
  1.2 0.0 copy-done.2
  1.2 27.1 %shard_map.46 = bf16[1,512,1024]{2,1,0:T(8,128)(2,1)S(1)} custom-call(s32[8,128]{1,0:T(8,128)S(1)} %bitcast.7, s32[2,1024]{1,0:T(2,128)S(1)} %copy-done.1, bf16[2,256,512]{2,1,0:T(8,128)(2,1)S(1)} %bitcast.6, bf16[2,256,512]{2,1,0:T(8,128)(2,1)S(1)} %copy-done), custom_call_target="tpu_custom_call" | custom-call | flops 2684354560 | bytes 2097152 | tf_op jit(solution)/shard_map/pallas_call | solution.py:438
  28.3 1.0 %copy.9 = bf16[1,512,1024]{2,1,0:T(8,128)(2,1)} copy(bf16[1,512,1024]{2,1,0:T(8,128)(2,1)S(1)} %shard_map.46) | data formatting | bytes 2097152
Async XLA Ops:
  0.0 1.2 %copy-start = (bf16[2,256,512]{2,1,0:T(8,128)(2,1)S(1)}, bf16[2,256,512]{2,1,0:T(8,128)(2,1)}, u32[]{:S(2)}) copy-start(bf16[2,256,512]{2,1,0:T(8,128)(2,1)} %inv_ref.1) | copy-start | bytes 1572868
  0.0 1.2 %copy-start.1 = (s32[2,1024]{1,0:T(2,128)S(1)}, s32[2,1024]{1,0:T(2,128)}, u32[]{:S(2)}) copy-start(s32[2,1024]{1,0:T(2,128)} %pred_ref.1) | copy-start | bytes 24580
  0.0 1.2 %copy-start.2 = (s32[2,1,512]{2,1,0:T(1,128)S(1)}, s32[2,1,512]{2,1,0:T(1,128)}, u32[]{:S(2)}) copy-start(s32[2,1,512]{2,1,0:T(1,128)} %param.4) | copy-start | bytes 12292

commit v5 on v4

--- a/solution.py
+++ b/solution.py
@@ -176,7 +176,10 @@
 
         @pl.when(is_second & (c == source))
         def _():
-            for copy in sends:
+            near = sends[LANES * n_rhs:]
+            for n, copy in enumerate(sends[:LANES * n_rhs]):
+                if n < len(near):
+                    near[n].start()
                 copy.start()
 
     step = q // PIECES

time: 29.4 us -> 29.4 us (level)
  no operation moved by 1% of the time
where the time goes in v5:
time: 29.4 us; the launch traced here: 29.3 us
  Pallas kernels  27.1 us (92%)
  local copies, waits for them, and re-layouts  2.17 us (7%)
    pallas_call x1, Pallas kernels, on_device(): pl.pallas_call(functools.partial(kernel, n_rows, n_rhs), out_shape=jax.Sh...  27.1 us
    unnamed x8, local copies, waits for them, and re-layouts  2.17 us

profile of v5, /device:TPU:9, one launch (start us, length us, event | category | flops | bytes accessed | tf_op | source)
XLA Modules:
  0.0 29.3 jit_solution(3483692765736084221)
XLA Ops:
  0.0 0.0 copy-start
  0.0 0.0 copy-start.1
  0.0 0.0 copy-start.2
  0.0 1.2 %copy.7 = bf16[1,256,2,512]{3,1,2,0:T(8,128)(2,1)S(1)} copy(bf16[1,256,2,512]{3,2,1,0:T(2,128)(2,1)} %param.6) | data formatting | bytes 1048576 | tf_op args[2]
  1.2 0.0 copy-done
  1.2 0.0 copy-done.1
  1.2 0.0 copy-done.2
  1.2 27.1 %shard_map.46 = bf16[1,512,1024]{2,1,0:T(8,128)(2,1)S(1)} custom-call(s32[8,128]{1,0:T(8,128)S(1)} %bitcast.7, s32[2,1024]{1,0:T(2,128)S(1)} %copy-done.1, bf16[2,256,512]{2,1,0:T(8,128)(2,1)S(1)} %bitcast.6, bf16[2,256,512]{2,1,0:T(8,128)(2,1)S(1)} %copy-done), custom_call_target="tpu_custom_call" | custom-call | flops 2684354560 | bytes 2097152 | tf_op jit(solution)/shard_map/pallas_call | solution.py:441
  28.3 1.0 %copy.9 = bf16[1,512,1024]{2,1,0:T(8,128)(2,1)} copy(bf16[1,512,1024]{2,1,0:T(8,128)(2,1)S(1)} %shard_map.46) | data formatting | bytes 2097152
Async XLA Ops:
  0.0 1.2 %copy-start = (bf16[2,256,512]{2,1,0:T(8,128)(2,1)S(1)}, bf16[2,256,512]{2,1,0:T(8,128)(2,1)}, u32[]{:S(2)}) copy-start(bf16[2,256,512]{2,1,0:T(8,128)(2,1)} %inv_ref.1) | copy-start | bytes 1572868
  0.0 1.2 %copy-start.1 = (s32[2,1024]{1,0:T(2,128)S(1)}, s32[2,1024]{1,0:T(2,128)}, u32[]{:S(2)}) copy-start(s32[2,1024]{1,0:T(2,128)} %pred_ref.1) | copy-start | bytes 24580
  0.0 1.2 %copy-start.2 = (s32[2,1,512]{2,1,0:T(1,128)S(1)}, s32[2,1,512]{2,1,0:T(1,128)}, u32[]{:S(2)}) copy-start(s32[2,1,512]{2,1,0:T(1,128)} %param.4) | copy-start | bytes 12292
